TPU v7x, 256 devices: a whole 4x4x8 slice. The times are simulated.
256 devices in a mesh: seq: 32 (over y_hi, z, core), head: 8 (over y_lo, x).
Axes of the slice: x: 4, y: 4 (y_hi: 2, y_lo: 2; y = y_hi * 2 + y_lo), z: 8, core: 2. Of those that a mesh axis runs over, the one named last changes fastest.
Arguments:
- queries: bfloat16 [8192, 8192], P('seq', 'head'), parts along dimension 1, may hold values from -180 to 180
- keys: bfloat16 [8192, 1024], P('seq', 'head'), parts along dimension 1, may hold values from -6 to 6
- values: bfloat16 [8192, 1024], P('seq', 'head'), parts along dimension 1, may hold values from -6 to 6
- lengths: int32 [16], replicated, may hold values from 1 to 4608, 8192 in all
Outputs:
- attended: bfloat16 [8192, 8192], P('seq', 'head'), parts along dimension 1
There are 8 independent parts, one for each index of `head`. A program takes and returns all parts, laid end to end along the dimension named above; an argument that names none is the same for every part. Nothing has to cross between parts.
Inputs may be any that keep to these rules, and one draw needn't show every extreme that they name: Document lengths sum to 8192; the longest is exactly 4608.
All inputs are finite; a program needn't handle non-finite values.
Results may differ from a plain program's by a relative error of at most 0.0045.
Values may be sent and summed in bfloat16 or wider, within the bound.
A program may use at most 64 MiB of HBM per device.

v0:
```python
import math

import jax
import jax.numpy as jnp
from jax import lax
from jax.sharding import PartitionSpec as P

HQ = 8
DH = 128


def doc_index(positions, ends):
    return jnp.sum((positions[:, None] >= ends[None, :]).astype(jnp.int32), axis=1)


def local(queries, keys, values, lengths):
    rows = queries.shape[0]
    scale = 1.0 / math.sqrt(DH)
    ends = jnp.cumsum(lengths)
    position = lax.axis_index("seq")
    first_pos = position * rows
    query_pos = first_pos + jnp.arange(rows, dtype=jnp.int32)
    query_doc = doc_index(query_pos, ends)
    query_heads = queries.reshape(rows, HQ, DH)

    def absorb(carry, key_block, value_block, key_start):
        count = key_block.shape[0]
        top_old, total_old, acc_old = carry
        key_pos = key_start + jnp.arange(count, dtype=jnp.int32)
        key_doc = doc_index(key_pos, ends)
        allowed = (
            (key_pos[None, :] <= query_pos[:, None])
            & (key_doc[None, :] == query_doc[:, None])
            & (key_pos[None, :] >= 0)
        )
        scores = (
            jnp.einsum("thd,kd->thk", query_heads, key_block, preferred_element_type=jnp.float32)
            * scale
        )
        masked = jnp.where(allowed[:, None, :], scores, jnp.float32(-1e30))
        top_new = jnp.maximum(top_old, jnp.max(masked, axis=2))
        weights = jnp.where(
            allowed[:, None, :], jnp.exp(scores - top_new[:, :, None]), jnp.float32(0.0)
        )
        fade = jnp.exp(top_old - top_new)
        total_new = total_old * fade + jnp.sum(weights, axis=2)
        mixed = jnp.einsum(
            "thk,kd->thd",
            weights.astype(jnp.bfloat16),
            value_block,
            preferred_element_type=jnp.float32,
        )
        return (top_new, total_new, acc_old * fade[:, :, None] + mixed)

    init = (
        jnp.full((rows, HQ), -1e30, jnp.float32),
        jnp.zeros((rows, HQ), jnp.float32),
        jnp.zeros((rows, HQ, DH), jnp.float32),
    )
    key_piece = lax.all_gather(keys, "seq", axis=0, tiled=True)
    value_piece = lax.all_gather(values, "seq", axis=0, tiled=True)
    length = key_piece.shape[0]
    block = math.gcd(length, 512)
    key_blocks = key_piece.reshape(length // block, block, DH)
    value_blocks = value_piece.reshape(length // block, block, DH)

    def step_block(state, inputs):
        number, key_block, value_block = inputs
        return (absorb(state, key_block, value_block, number * block), None)

    numbers = jnp.arange(length // block, dtype=jnp.int32)
    result, unused = lax.scan(step_block, init, (numbers, key_blocks, value_blocks))
    carry = result
    top_final, total_final, acc_final = carry
    return (acc_final / total_final[:, :, None]).reshape(rows, HQ * DH).astype(jnp.bfloat16)


def solution(mesh):
    placed = (P("seq", "head"), P("seq", "head"), P("seq", "head"), P())
    return jax.shard_map(
        local, mesh=mesh, in_specs=placed, out_specs=P("seq", "head"), check_vma=False
    )
```

profile of v0, /device:TPU:23, one launch (start us, length us, event | category | flops | bytes accessed | tf_op | source)
XLA Modules:
  0.0 357.3 jit_solution(15573528913811153658)
XLA Ops:
  10.6 80.2 %all-gather.3.cloned.1.call-done = bf16[8192,128]{1,0:T(8,128)(2,1)} async-done(((bf16[256,128]{1,0:T(8,128)(2,1)}), bf16[8192,128]{1,0:T(8,128)(2,1)}) %all-gather.3.cloned.1.call-update) | async-done | bytes 2097168 | tf_op jit(solution)/shard_map/all_gather | solution.py:60
  90.8 79.3 %all-gather.5.cloned.1.call-done = bf16[8192,128]{1,0:T(8,128)(2,1)} async-done(((bf16[256,128]{1,0:T(8,128)(2,1)}), bf16[8192,128]{1,0:T(8,128)(2,1)}) %all-gather.5.cloned.1.call-update) | async-done | bytes 2097168 | tf_op jit(solution)/shard_map/all_gather | solution.py:61
  170.1 179.2 %while.15 = (s32[]{:T(128)}, f32[256,8]{0,1:T(8,128)S(1)}, f32[256,8]{0,1:T(8,128)S(1)}, f32[256,8,128]{2,0,1:T(8,128)S(1)}, s32[16]{0:T(128)S(1)}, /*index=5*/s...) while((s32[]{:T(128)}, f32[256,8]{0,1:T(8,128)S(1)}, ...), condition=%wide.region_6.7_spmd.clone, body=%wide.region_2.6_spmd.clone.sunk | while | flops 549752064 | bytes 32914704 | solution.py:72
  171.9 3.6 %fusion.36 = (f32[256,8]{0,1:T(8,128)S(1)}, f32[512,256,8]{1,0,2:T(8,128)}) fusion(pred[256,512]{0,1:T(8,128)(4,1)S(1)} %and_and_fusion.2, bf16[256,8,128]{2,0,1:T(8,128)(2,1)S(1)} %get-tuple-element.263, bf16[16,512,128]{2,1,0:T(8,128)(2,1)} %get-tuple-element.262, s32[]{:T(128)} %get-tuple-element.241), kind=kOutput, calls=%fused_computation.3.clone.1 | convolution fusion | flops 271579136 | bytes 4989440 | tf_op jit(solution)/shard_map/while/body/eval_jaxpr/thd,kd->thk/dot_general | solution.py:37
  175.5 3.2 fusion.37
  183.1 3.6 %fusion.36 = (f32[256,8]{0,1:T(8,128)S(1)}, f32[512,256,8]{1,0,2:T(8,128)}) fusion(pred[256,512]{0,1:T(8,128)(4,1)S(1)} %and_and_fusion.2, bf16[256,8,128]{2,0,1:T(8,128)(2,1)S(1)} %get-tuple-element.263, bf16[16,512,128]{2,1,0:T(8,128)(2,1)} %get-tuple-element.262, s32[]{:T(128)} %get-tuple-element.241), kind=kOutput, calls=%fused_computation.3.clone.1 | convolution fusion | flops 271579136 | bytes 4989440 | tf_op jit(solution)/shard_map/while/body/eval_jaxpr/thd,kd->thk/dot_general | solution.py:37
  186.7 3.2 fusion.37
  194.3 3.6 %fusion.36 = (f32[256,8]{0,1:T(8,128)S(1)}, f32[512,256,8]{1,0,2:T(8,128)}) fusion(pred[256,512]{0,1:T(8,128)(4,1)S(1)} %and_and_fusion.2, bf16[256,8,128]{2,0,1:T(8,128)(2,1)S(1)} %get-tuple-element.263, bf16[16,512,128]{2,1,0:T(8,128)(2,1)} %get-tuple-element.262, s32[]{:T(128)} %get-tuple-element.241), kind=kOutput, calls=%fused_computation.3.clone.1 | convolution fusion | flops 271579136 | bytes 4989440 | tf_op jit(solution)/shard_map/while/body/eval_jaxpr/thd,kd->thk/dot_general | solution.py:37
  197.9 3.2 fusion.37
  205.5 3.6 %fusion.36 = (f32[256,8]{0,1:T(8,128)S(1)}, f32[512,256,8]{1,0,2:T(8,128)}) fusion(pred[256,512]{0,1:T(8,128)(4,1)S(1)} %and_and_fusion.2, bf16[256,8,128]{2,0,1:T(8,128)(2,1)S(1)} %get-tuple-element.263, bf16[16,512,128]{2,1,0:T(8,128)(2,1)} %get-tuple-element.262, s32[]{:T(128)} %get-tuple-element.241), kind=kOutput, calls=%fused_computation.3.clone.1 | convolution fusion | flops 271579136 | bytes 4989440 | tf_op jit(solution)/shard_map/while/body/eval_jaxpr/thd,kd->thk/dot_general | solution.py:37
  209.1 3.2 fusion.37
  216.7 3.6 %fusion.36 = (f32[256,8]{0,1:T(8,128)S(1)}, f32[512,256,8]{1,0,2:T(8,128)}) fusion(pred[256,512]{0,1:T(8,128)(4,1)S(1)} %and_and_fusion.2, bf16[256,8,128]{2,0,1:T(8,128)(2,1)S(1)} %get-tuple-element.263, bf16[16,512,128]{2,1,0:T(8,128)(2,1)} %get-tuple-element.262, s32[]{:T(128)} %get-tuple-element.241), kind=kOutput, calls=%fused_computation.3.clone.1 | convolution fusion | flops 271579136 | bytes 4989440 | tf_op jit(solution)/shard_map/while/body/eval_jaxpr/thd,kd->thk/dot_general | solution.py:37
  220.3 3.2 fusion.37
  227.9 3.6 %fusion.36 = (f32[256,8]{0,1:T(8,128)S(1)}, f32[512,256,8]{1,0,2:T(8,128)}) fusion(pred[256,512]{0,1:T(8,128)(4,1)S(1)} %and_and_fusion.2, bf16[256,8,128]{2,0,1:T(8,128)(2,1)S(1)} %get-tuple-element.263, bf16[16,512,128]{2,1,0:T(8,128)(2,1)} %get-tuple-element.262, s32[]{:T(128)} %get-tuple-element.241), kind=kOutput, calls=%fused_computation.3.clone.1 | convolution fusion | flops 271579136 | bytes 4989440 | tf_op jit(solution)/shard_map/while/body/eval_jaxpr/thd,kd->thk/dot_general | solution.py:37
  239.1 3.6 %fusion.36 = (f32[256,8]{0,1:T(8,128)S(1)}, f32[512,256,8]{1,0,2:T(8,128)}) fusion(pred[256,512]{0,1:T(8,128)(4,1)S(1)} %and_and_fusion.2, bf16[256,8,128]{2,0,1:T(8,128)(2,1)S(1)} %get-tuple-element.263, bf16[16,512,128]{2,1,0:T(8,128)(2,1)} %get-tuple-element.262, s32[]{:T(128)} %get-tuple-element.241), kind=kOutput, calls=%fused_computation.3.clone.1 | convolution fusion | flops 271579136 | bytes 4989440 | tf_op jit(solution)/shard_map/while/body/eval_jaxpr/thd,kd->thk/dot_general | solution.py:37
  250.3 3.6 %fusion.36 = (f32[256,8]{0,1:T(8,128)S(1)}, f32[512,256,8]{1,0,2:T(8,128)}) fusion(pred[256,512]{0,1:T(8,128)(4,1)S(1)} %and_and_fusion.2, bf16[256,8,128]{2,0,1:T(8,128)(2,1)S(1)} %get-tuple-element.263, bf16[16,512,128]{2,1,0:T(8,128)(2,1)} %get-tuple-element.262, s32[]{:T(128)} %get-tuple-element.241), kind=kOutput, calls=%fused_computation.3.clone.1 | convolution fusion | flops 271579136 | bytes 4989440 | tf_op jit(solution)/shard_map/while/body/eval_jaxpr/thd,kd->thk/dot_general | solution.py:37
  261.5 3.6 %fusion.36 = (f32[256,8]{0,1:T(8,128)S(1)}, f32[512,256,8]{1,0,2:T(8,128)}) fusion(pred[256,512]{0,1:T(8,128)(4,1)S(1)} %and_and_fusion.2, bf16[256,8,128]{2,0,1:T(8,128)(2,1)S(1)} %get-tuple-element.263, bf16[16,512,128]{2,1,0:T(8,128)(2,1)} %get-tuple-element.262, s32[]{:T(128)} %get-tuple-element.241), kind=kOutput, calls=%fused_computation.3.clone.1 | convolution fusion | flops 271579136 | bytes 4989440 | tf_op jit(solution)/shard_map/while/body/eval_jaxpr/thd,kd->thk/dot_general | solution.py:37
  272.7 3.6 %fusion.36 = (f32[256,8]{0,1:T(8,128)S(1)}, f32[512,256,8]{1,0,2:T(8,128)}) fusion(pred[256,512]{0,1:T(8,128)(4,1)S(1)} %and_and_fusion.2, bf16[256,8,128]{2,0,1:T(8,128)(2,1)S(1)} %get-tuple-element.263, bf16[16,512,128]{2,1,0:T(8,128)(2,1)} %get-tuple-element.262, s32[]{:T(128)} %get-tuple-element.241), kind=kOutput, calls=%fused_computation.3.clone.1 | convolution fusion | flops 271579136 | bytes 4989440 | tf_op jit(solution)/shard_map/while/body/eval_jaxpr/thd,kd->thk/dot_general | solution.py:37
  283.9 3.6 %fusion.36 = (f32[256,8]{0,1:T(8,128)S(1)}, f32[512,256,8]{1,0,2:T(8,128)}) fusion(pred[256,512]{0,1:T(8,128)(4,1)S(1)} %and_and_fusion.2, bf16[256,8,128]{2,0,1:T(8,128)(2,1)S(1)} %get-tuple-element.263, bf16[16,512,128]{2,1,0:T(8,128)(2,1)} %get-tuple-element.262, s32[]{:T(128)} %get-tuple-element.241), kind=kOutput, calls=%fused_computation.3.clone.1 | convolution fusion | flops 271579136 | bytes 4989440 | tf_op jit(solution)/shard_map/while/body/eval_jaxpr/thd,kd->thk/dot_general | solution.py:37
  295.1 3.6 %fusion.36 = (f32[256,8]{0,1:T(8,128)S(1)}, f32[512,256,8]{1,0,2:T(8,128)}) fusion(pred[256,512]{0,1:T(8,128)(4,1)S(1)} %and_and_fusion.2, bf16[256,8,128]{2,0,1:T(8,128)(2,1)S(1)} %get-tuple-element.263, bf16[16,512,128]{2,1,0:T(8,128)(2,1)} %get-tuple-element.262, s32[]{:T(128)} %get-tuple-element.241), kind=kOutput, calls=%fused_computation.3.clone.1 | convolution fusion | flops 271579136 | bytes 4989440 | tf_op jit(solution)/shard_map/while/body/eval_jaxpr/thd,kd->thk/dot_general | solution.py:37
  306.3 3.6 %fusion.36 = (f32[256,8]{0,1:T(8,128)S(1)}, f32[512,256,8]{1,0,2:T(8,128)}) fusion(pred[256,512]{0,1:T(8,128)(4,1)S(1)} %and_and_fusion.2, bf16[256,8,128]{2,0,1:T(8,128)(2,1)S(1)} %get-tuple-element.263, bf16[16,512,128]{2,1,0:T(8,128)(2,1)} %get-tuple-element.262, s32[]{:T(128)} %get-tuple-element.241), kind=kOutput, calls=%fused_computation.3.clone.1 | convolution fusion | flops 271579136 | bytes 4989440 | tf_op jit(solution)/shard_map/while/body/eval_jaxpr/thd,kd->thk/dot_general | solution.py:37
  317.5 3.6 %fusion.36 = (f32[256,8]{0,1:T(8,128)S(1)}, f32[512,256,8]{1,0,2:T(8,128)}) fusion(pred[256,512]{0,1:T(8,128)(4,1)S(1)} %and_and_fusion.2, bf16[256,8,128]{2,0,1:T(8,128)(2,1)S(1)} %get-tuple-element.263, bf16[16,512,128]{2,1,0:T(8,128)(2,1)} %get-tuple-element.262, s32[]{:T(128)} %get-tuple-element.241), kind=kOutput, calls=%fused_computation.3.clone.1 | convolution fusion | flops 271579136 | bytes 4989440 | tf_op jit(solution)/shard_map/while/body/eval_jaxpr/thd,kd->thk/dot_general | solution.py:37
  328.7 3.6 %fusion.36 = (f32[256,8]{0,1:T(8,128)S(1)}, f32[512,256,8]{1,0,2:T(8,128)}) fusion(pred[256,512]{0,1:T(8,128)(4,1)S(1)} %and_and_fusion.2, bf16[256,8,128]{2,0,1:T(8,128)(2,1)S(1)} %get-tuple-element.263, bf16[16,512,128]{2,1,0:T(8,128)(2,1)} %get-tuple-element.262, s32[]{:T(128)} %get-tuple-element.241), kind=kOutput, calls=%fused_computation.3.clone.1 | convolution fusion | flops 271579136 | bytes 4989440 | tf_op jit(solution)/shard_map/while/body/eval_jaxpr/thd,kd->thk/dot_general | solution.py:37
  339.9 3.6 %fusion.36 = (f32[256,8]{0,1:T(8,128)S(1)}, f32[512,256,8]{1,0,2:T(8,128)}) fusion(pred[256,512]{0,1:T(8,128)(4,1)S(1)} %and_and_fusion.2, bf16[256,8,128]{2,0,1:T(8,128)(2,1)S(1)} %get-tuple-element.263, bf16[16,512,128]{2,1,0:T(8,128)(2,1)} %get-tuple-element.262, s32[]{:T(128)} %get-tuple-element.241), kind=kOutput, calls=%fused_computation.3.clone.1 | convolution fusion | flops 271579136 | bytes 4989440 | tf_op jit(solution)/shard_map/while/body/eval_jaxpr/thd,kd->thk/dot_general | solution.py:37
  (219 shorter events, 98.4 us)
Async XLA Ops:
  6.5 84.2 %all-gather.3.cloned.1.call-start = ((), (), s32[]{:S(2)}) async-start(), calls=%async_computation | async-start | bytes 2162688 | tf_op jit(solution)/shard_map/all_gather | solution.py:60
  7.3 162.8 %all-gather.5.cloned.1.call-start = ((), (), s32[]{:S(2)}) async-start(), calls=%async_computation.1 | async-start | bytes 2162688 | tf_op jit(solution)/shard_map/all_gather | solution.py:61
  175.5 3.4 copy-start
  186.7 3.4 copy-start
  197.9 3.4 copy-start
  209.1 3.4 copy-start
  220.3 3.4 copy-start
  231.5 3.4 copy-start
  242.7 3.4 copy-start
  253.9 3.4 copy-start
  265.1 3.4 copy-start
  276.3 3.4 copy-start
  287.5 3.4 copy-start
  298.7 3.4 copy-start
  309.9 3.4 copy-start
  321.1 3.4 copy-start
  332.3 3.4 copy-start
  343.5 3.4 copy-start
Sparse Core Ops, SparseCore 0:
  10.1 80.5 all-gather.2
  93.5 76.5 all-gather.4
where the time goes:
time: 362 us; the launch traced here: 357 us
  waiting for transfers between devices  161 us (44%)
  matrix products  95.4 us (26%)
  other arithmetic  58.8 us (16%)
  local copies, waits for them, and re-layouts  16.5 us (5%)
  between operations  13.5 us (4%)
  loops' own time  12.1 us (3%)
    all_gather x1, waiting for transfers between devices, local(): key_piece = lax.all_gather(keys, 'seq', axis=0, tiled=True)  80.2 us
    all_gather x1, waiting for transfers between devices, local(): value_piece = lax.all_gather(values, 'seq', axis=0, tiled=True)  79.3 us
    dot_general x16, matrix products, absorb(): jnp.einsum('thd,kd->thk', query_heads, key_block, preferred_element_type=...  57.7 us
    reduce_sum x16, other arithmetic, absorb(): total_new = total_old * fade + jnp.sum(weights, axis=2)  51.2 us
    dot_general x16, matrix products, absorb(): jnp.einsum('thk,kd->thd', weights.astype(jnp.bfloat16), value_block, pref...  37.6 us
    another operation x1, loops' own time, local(): lax.scan(step_block, init, (numbers, key_blocks, value_blocks))  12.1 us
    dynamic_slice x16, local copies, waits for them, and re-layouts, local(): lax.scan(step_block, init, (numbers, key_blocks, value_blocks))  10.7 us
  transfers between devices with their start and end apart: 2, of which 2 were waited for; matrix products, arithmetic and copies ran while one was open for 1% of the time, Pallas kernels for 0%

commit v1 on v0

v1 whole, which is shorter than its diff:
```python
import functools
import math

import jax
import jax.numpy as jnp
from jax import lax
from jax.experimental import pallas as pl
from jax.experimental.pallas import tpu as pltpu
from jax.sharding import PartitionSpec as P

MESH = pl.DeviceIdType.MESH
HQ = 8
DH = 128
NDOC = 16
ROWS = 256
CHIPS = 16
CHUNKS = 4
PART = ROWS // CHUNKS
ROUNDS = 4
NONE = 31
FAR = -(2.0**20)
SCALE = math.log2(math.e) / math.sqrt(DH)

IN_WORDS = (
    (31969, 65504, 64833, 65506, 65507, 65508, 65509, 97472, 64800, 100392, 97385, 97418, 97451, 97484, 97517, 97736),
    (32767, 32746, 65504, 65505, 65506, 65507, 97284, 97441, 97506, 97376, 99464, 101545, 101578, 102635, 103692, 104873),
    (31818, 32767, 32767, 65504, 65505, 97282, 97315, 65508, 99523, 97415, 97442, 100552, 102633, 103690, 104747, 71047),
    (32767, 32767, 32767, 32767, 65504, 65505, 65506, 97378, 97444, 97446, 97479, 65511, 65512, 65513, 65514, 97611),
)
OUT_WORDS = (
    (1015808, 1016865, 98274, 131043, 163812, 196581, 229350, 262119, 1047816, 1047849, 1027050, 1048555, 1048556, 1048557, 1048558, 1048575),
    (1023039, 1048544, 1017153, 1019874, 1019875, 1020900, 1021925, 1021983, 1047840, 1047624, 1047657, 1047690, 1047723, 1047756, 1047789, 1047839),
    (1017855, 1047903, 1048544, 1018849, 1020898, 1021923, 1021956, 1020991, 1018087, 1047650, 1047688, 1047721, 1047754, 1047787, 1047820, 1047846),
    (359519, 1048575, 1048575, 1048544, 1048545, 1048546, 1048547, 1048575, 1048550, 1047687, 1047743, 1047752, 1047785, 1048554, 1048555, 1048549),
)

NT = (((1,), (1,)), ((), ()))


def pick(table, index, default=None):
    value = jnp.int32(table[0]) if default is None else jnp.int32(default)
    for number in range(0 if default is not None else 1, len(table)):
        value = jnp.where(index == number, table[number], value)
    return value


def field(word, place):
    return (word // 32**place) % 32


def kernel(
    queries_hbm, keys_hbm, values_hbm, lengths_ref, out_ref,
    q_ref, kv, far, mine, top, acc,
    q_sem, own_sem, recv_sem, sib_recv, send_sem, sib_send,
):
    seq, head = lax.axis_index("seq"), lax.axis_index("head")
    core = seq % 2
    chip = seq // 2
    z = chip % 8
    high = chip // 8
    own = 2 * chip + core

    def device(high, z, core):
        return (high * 16 + ((z + 8) % 8) * 2 + core, head)

    sibling = device(high, z, 1 - core)
    across = device(1 - high, z, core)
    slant = device(1 - high, z - 1 + 2 * high, core)
    edges = (device(high, z + 1, core), device(high, z - 1, core), across, slant)

    barrier = pltpu.get_barrier_semaphore()
    for other in edges + (sibling,):
        pl.semaphore_signal(barrier, inc=1, device_id=other, device_id_type=MESH)

    load_q = pltpu.make_async_copy(queries_hbm, q_ref, q_sem)
    load_q.start()
    for chunk in range(CHUNKS):
        part = pl.ds(chunk * PART, PART)
        pltpu.make_async_copy(keys_hbm.at[part], kv.at[own, chunk, 0], own_sem).start()
        pltpu.make_async_copy(values_hbm.at[part], kv.at[own, chunk, 1], own_sem).start()

    ins = [pick(row, chip) for row in IN_WORDS]
    outs = [pick(row, chip) for row in OUT_WORDS]

    lane = lax.broadcasted_iota(jnp.int32, (1, DH), 1)
    first = jnp.zeros((1, DH), jnp.int32)
    last = jnp.zeros((1, DH), jnp.int32)
    begin = jnp.int32(0)
    for number in range(NDOC):
        end = begin + lengths_ref[number]
        first = jnp.where(lane == number, begin, first)
        last = jnp.where(lane == number, end, last)
        begin = end

    row_pos = own * ROWS + lax.broadcasted_iota(jnp.int32, (ROWS, DH), 0)
    mine[...] = ((row_pos >= first) & (row_pos < last)).astype(jnp.float32).astype(jnp.bfloat16)

    @pl.loop(0, CHIPS)
    def _(block):
        pos = block * 2 * ROWS + lax.broadcasted_iota(jnp.int32, (2 * ROWS, DH), 0)
        inside = (pos >= first) & (pos < last)
        far[block] = jnp.where(inside | (lane >= NDOC), 0.0, FAR).astype(jnp.bfloat16)

    pltpu.make_async_copy(kv.at[own], kv.at[own], own_sem).wait()
    pl.semaphore_wait(barrier, 5)

    def sib_copy(block, chunk, sem):
        part = kv.at[2 * block + core, chunk]
        return pltpu.make_async_remote_copy(
            src_ref=part, dst_ref=part, send_sem=sem, recv_sem=sib_recv.at[block],
            device_id=sibling, device_id_type=MESH,
        )

    def sib_whole(block, sem):
        part = kv.at[2 * block + 1 - core]
        return pltpu.make_async_remote_copy(
            src_ref=part, dst_ref=part, send_sem=sem, recv_sem=sib_recv.at[block],
            device_id=sibling, device_id_type=MESH,
        )

    def edge_copy(edge, block, chunk, sem):
        part = kv.at[2 * block + core, chunk]
        return pltpu.make_async_remote_copy(
            src_ref=part, dst_ref=part, send_sem=sem, recv_sem=recv_sem.at[block, chunk],
            device_id=edges[edge], device_id_type=MESH,
        )

    def receive(number, word, chunk):
        needed = word // 32768
        for place in range(3):
            block = field(word, place)

            @pl.when(block < CHIPS)
            def _():
                edge_copy(0, block, chunk, send_sem.at[0, 0]).wait_recv()

            @pl.when(place < needed)
            def _():
                sib_copy(block, chunk, sib_send.at[number, place]).start()

    def forward(number, word, chunk):
        for edge in range(4):
            block = field(word, edge)

            @pl.when(block < CHIPS)
            def _():
                edge_copy(edge, block, chunk, send_sem.at[number, edge]).start()

    for chunk in range(CHUNKS):
        forward(0, outs[0], chunk)
    for chunk in range(CHUNKS):
        sib_copy(chip, chunk, sib_send.at[ROUNDS, 0]).start()

    def load_keys(block):
        both = kv[pl.ds(2 * block, 2), :, 0].reshape(2 * ROWS, DH)
        return jnp.concatenate([both, far[block]], axis=1)

    def load_values(block):
        both = kv[pl.ds(2 * block, 2), :, 1].reshape(2 * ROWS, DH)
        return jnp.concatenate([both, jnp.ones_like(both)], axis=1)

    def load_queries(h):
        return jnp.concatenate([q_ref[:, pl.ds(pl.multiple_of(h * DH, DH), DH)], mine[...]], axis=1)

    def wide(x, count):
        return jnp.concatenate([x] * count, axis=1)

    load_q.wait()
    sib_whole(chip, sib_send.at[ROUNDS, 0]).wait_recv()

    @pl.loop(0, 2)
    def _(half):
        keys, values = load_keys(chip), load_values(chip)
        shape = (ROWS, 2 * ROWS)
        key_pos = lax.broadcasted_iota(jnp.int32, shape, 1)
        causal = key_pos <= core * ROWS + lax.broadcasted_iota(jnp.int32, shape, 0)
        for i in range(HQ // 2):
            h = half * (HQ // 2) + i
            scores = lax.dot_general(load_queries(h), keys, NT, preferred_element_type=jnp.float32)
            scores = jnp.where(causal, scores, -1e30)
            peak = jnp.broadcast_to(jnp.max(scores, axis=1, keepdims=True), (ROWS, DH))
            top[h] = peak
            weights = jnp.exp2((scores - wide(peak, 4)) * SCALE).astype(jnp.bfloat16)
            acc[h] = jnp.dot(weights, values, preferred_element_type=jnp.float32)

    for chunk in range(CHUNKS):
        receive(0, ins[0], chunk)
        forward(1, outs[1], chunk)

    def absorb(blocks, half):
        count = len(blocks)
        keys = jnp.concatenate([load_keys(b) for b in blocks], axis=0)
        values = jnp.concatenate([load_values(b) for b in blocks], axis=0)
        number = HQ // 2
        kept = {}
        for step in range(number + 1):
            if step < number:
                h = half * number + step
                scores = lax.dot_general(load_queries(h), keys, NT, preferred_element_type=jnp.float32)
                old = top[h]
                new = jnp.maximum(old, jnp.max(scores, axis=1, keepdims=True))
                top[h] = new
                fade = jnp.exp2((old - new) * SCALE)
                weights = jnp.exp2((scores - wide(new, 4 * count)) * SCALE).astype(jnp.bfloat16)
                kept[step] = (fade, weights)
            if step >= 1:
                h = half * number + step - 1
                fade, weights = kept.pop(step - 1)
                acc[h] = acc[h] * wide(fade, 2) + jnp.dot(
                    weights, values, preferred_element_type=jnp.float32
                )

    @pl.loop(0, 2 * ROUNDS)
    def _(step):
        number, half = step // 2, step % 2
        arrived = pick(ins, number + 1, 32767)
        leaving = pick(outs, number + 2, 1048575)
        for i in range(CHUNKS // 2):
            chunk = half * (CHUNKS // 2) + i
            receive(number + 1, arrived, chunk)
            forward(number + 2, leaving, chunk)

        word = pick(ins, number, 32767)
        needed = word // 32768
        blocks = [field(word, place) for place in range(3)]

        @pl.when(half == 0)
        def _():
            for place in range(3):
                @pl.when(place < needed)
                def _():
                    sib_whole(blocks[place], sib_send.at[0, 0]).wait_recv()

        for count in range(1, 4):
            @pl.when(needed == count)
            def _():
                absorb(blocks[:count], half)

    for h in range(HQ):
        out_ref[:, h * DH:(h + 1) * DH] = (acc[h, :, :DH] / acc[h, :, DH:]).astype(jnp.bfloat16)

    sib_whole(chip, sib_send.at[ROUNDS, 0]).wait_send()
    for number in range(ROUNDS):
        for place in range(3):
            @pl.when(place < ins[number] // 32768)
            def _():
                sib_whole(chip, sib_send.at[number, place]).wait_send()
        for edge in range(4):
            block = field(outs[number], edge)

            @pl.when(block < CHIPS)
            def _():
                sib_whole(chip, send_sem.at[number, edge]).wait_send()


def local(queries, keys, values, lengths):
    anywhere = pl.BlockSpec(memory_space=pl.ANY)
    return pl.pallas_call(
        kernel,
        out_shape=jax.ShapeDtypeStruct(queries.shape, jnp.bfloat16),
        in_specs=[anywhere] * 3 + [pl.BlockSpec(memory_space=pltpu.SMEM)],
        out_specs=pl.BlockSpec(memory_space=pltpu.VMEM),
        scratch_shapes=[
            pltpu.VMEM((ROWS, HQ * DH), jnp.bfloat16),
            pltpu.VMEM((2 * CHIPS, CHUNKS, 2, PART, DH), jnp.bfloat16),
            pltpu.VMEM((CHIPS, 2 * ROWS, DH), jnp.bfloat16),
            pltpu.VMEM((ROWS, DH), jnp.bfloat16),
            pltpu.VMEM((HQ, ROWS, DH), jnp.float32),
            pltpu.VMEM((HQ, ROWS, 2 * DH), jnp.float32),
            pltpu.SemaphoreType.DMA,
            pltpu.SemaphoreType.DMA,
            pltpu.SemaphoreType.DMA((CHIPS, CHUNKS)),
            pltpu.SemaphoreType.DMA((CHIPS,)),
            pltpu.SemaphoreType.DMA((ROUNDS, 4)),
            pltpu.SemaphoreType.DMA((ROUNDS + 1, 3)),
        ],
        compiler_params=pltpu.CompilerParams(
            collective_id=0, has_side_effects=True, vmem_limit_bytes=56 * 2**20
        ),
    )(queries, keys, values, lengths)


def solution(mesh):
    placed = (P("seq", "head"), P("seq", "head"), P("seq", "head"), P())
    return jax.shard_map(
        local, mesh=mesh, in_specs=placed, out_specs=P("seq", "head"), check_vma=False
    )
```

time: 362 us -> 35.5 us (0.10)
  the two profiles are of different devices: /device:TPU:23 before, /device:TPU:16 now
where the time goes in v1:
time: 35.5 us; the launch traced here: 35.4 us
  Pallas kernels  33.5 us (94%)
  local copies, waits for them, and re-layouts  1.87 us (5%)
    pallas_call x1, Pallas kernels, local(): pl.pallas_call(kernel, out_shape=jax.ShapeDtypeStruct(queries.shape, jnp....  33.5 us
    unnamed x1, local copies, waits for them, and re-layouts  1.87 us

profile of v1, /device:TPU:16, one launch (start us, length us, event | category | flops | bytes accessed | tf_op | source)
XLA Modules:
  0.0 35.4 jit_solution(11157702287202447689)
XLA Ops:
  0.0 33.5 %shard_map.46 = bf16[256,1024]{1,0:T(8,128)(2,1)} custom-call(bf16[256,1024]{1,0:T(8,128)(2,1)} %queries_hbm.1, bf16[256,128]{1,0:T(8,128)(2,1)} %keys_hbm.1, bf16[256,128]{1,0:T(8,128)(2,1)} %values_hbm.1, s32[16]{0:T(128)} %lengths_ref.1), custom_call_target="tpu_custom_call" | custom-call | tf_op jit(solution)/shard_map/pallas_call | solution.py:258
  33.5 1.9 %copy.6 = bf16[256,1024]{1,0:T(8,128)(2,1)} copy(bf16[256,1024]{1,0:T(8,128)(2,1)} %shard_map.46) | data formatting | bytes 1048576

commit v2 on v0

v2 whole, which is shorter than its diff:
```python
import math

import jax
import jax.numpy as jnp
from jax import lax
from jax.experimental import pallas as pl
from jax.experimental.pallas import tpu as pltpu
from jax.sharding import PartitionSpec as P

MESH = pl.DeviceIdType.MESH
HQ = 8
DH = 128
NDOC = 16
ROWS = 256
CHIPS = 16
HALF = ROWS // 2
FAR = -(2.0**20)
SCALE = math.log2(math.e) / math.sqrt(DH)
REACH = 9
LIMIT = 2.0**100
PIECE = 64

FIRST = 3
WORK_WORDS = (
    (0, 0, 32771, 32772, 32774, 32777, 65856, 32780, 32768, 65616, 65683, 65748, 65846, 65880, 66384, 66044),
    (0, 0, 32770, 32773, 0, 32775, 0, 32770, 32769, 32785, 32773, 65778, 32791, 0, 66348, 66482),
    (0, 32768, 0, 0, 32773, 32776, 32769, 32779, 0, 65637, 32785, 0, 66221, 65913, 66091, 66413),
    (0, 32769, 0, 32771, 32775, 32768, 0, 32777, 65667, 65728, 66054, 66154, 66184, 66070, 66221, 32782),
    (0, 0, 0, 32770, 0, 32772, 65763, 32778, 65996, 65761, 65993, 66212, 65930, 66280, 65880, 66067),
    (0, 0, 32768, 0, 32772, 32769, 65605, 65574, 66018, 65679, 65810, 65705, 66002, 66124, 66043, 66362),
    (0, 0, 0, 32769, 65539, 32773, 32779, 65677, 65704, 65832, 65763, 65969, 65739, 65967, 66254, 66092),
    (0, 0, 32769, 0, 32770, 65638, 65832, 65768, 65901, 65870, 65922, 66056, 65779, 66101, 66290, 66197),
    (0, 0, 0, 32768, 32769, 32770, 65732, 65699, 65830, 65933, 65898, 65900, 66096, 66153, 66195, 66264),
    (0, 0, 0, 0, 0, 0, 0, 32768, 65863, 32779, 65967, 66030, 32783, 66190, 0, 32791),
)
IN_WORDS = (
    (32771, 118214, 163843, 252164, 196998, 163849, 328000, 163852, 197280, 327760, 327827, 327892, 327990, 328024, 504656, 328188),
    (0, 32783, 196866, 163845, 0, 163847, 32782, 163842, 163841, 197265, 163845, 327922, 163863, 0, 163865, 328626),
    (0, 196736, 0, 0, 163845, 197032, 163841, 163851, 32788, 327781, 163857, 0, 500397, 328057, 505387, 506733),
    (0, 197313, 0, 196963, 163847, 163840, 0, 163849, 503939, 327872, 501254, 496234, 504148, 328214, 502549, 0),
    (0, 32780, 0, 163842, 0, 163844, 327907, 163850, 506958, 507105, 500302, 496949, 163858, 504552, 506363, 518675),
    (0, 0, 163840, 0, 163844, 163841, 502853, 504870, 505000, 163844, 493795, 500145, 498030, 505330, 0, 360857),
    (0, 0, 0, 163841, 327683, 163845, 0, 327940, 327883, 506152, 328012, 503184, 327923, 501301, 328278, 328369),
    (0, 0, 163841, 0, 163842, 327782, 327976, 163847, 0, 504234, 328171, 163854, 163856, 328147, 328311, 328468),
    (0, 0, 0, 163840, 163841, 163842, 327876, 491683, 327913, 0, 163853, 163855, 328177, 163860, 163860, 328438),
    (0, 0, 0, 0, 0, 0, 0, 0, 163850, 163851, 0, 0, 0, 0, 0, 0),
)
OUT_WORDS = (
    (268550144, 461915747, 268552292, 462949478, 463753321, 268555370, 464525420, 268557966, 268443760, 268559987, 268446324, 268561526, 134217848, 134217850, 134217852, 0),
    (134217953, 268436578, 454412901, 268553863, 134217736, 134217995, 268524301, 268508718, 134217841, 268444818, 134217780, 134217847, 134217881, 0, 134217853, 0),
    (268436064, 268535523, 268503588, 134217926, 268554344, 447338123, 268556845, 134217966, 268444305, 0, 268445845, 0, 134217849, 134217883, 0, 0),
    (134217825, 449715430, 134217827, 462433383, 268570860, 268441225, 268555296, 134217998, 268446304, 134217840, 268437619, 134217844, 268440182, 268457080, 268507184, 0),
    (134217731, 134217967, 446812258, 268552836, 0, 134217831, 448388202, 134217868, 268460129, 268452978, 134217845, 268439154, 268456567, 134217851, 268458106, 268459631),
    (0, 268438624, 268538082, 268554340, 268553349, 134217965, 268452449, 472766498, 134217760, 268454499, 268454001, 268510247, 134217773, 134217771, 268555897, 464789101),
    (0, 465045633, 0, 455988835, 268553829, 463802400, 0, 0, 268507185, 134217766, 268456560, 268457075, 268458101, 134217846, 268460661, 134217778),
    (0, 450484321, 0, 134217826, 134217830, 134217832, 268453479, 268571177, 0, 268445807, 134217838, 268440723, 0, 268460151, 268459128, 268507699),
    (0, 134217731, 134217824, 134217899, 0, 268452452, 268452965, 268571686, 134217748, 268508711, 0, 268458609, 134217844, 268512815, 0, 134217952),
)
EDGES = ((-2, 0), (-2, 1), (-1, 0), (-1, 1), (0, 1), (1, 0), (1, 1), (2, 0))

NT = (((1,), (1,)), ((), ()))


def pick(table, index, default):
    value = jnp.int32(default)
    for number, entry in enumerate(table):
        value = jnp.where(index == number, entry, value)
    return value


def kernel(
    queries_hbm, keys_hbm, values_hbm, lengths_hbm, out_hbm, over_hbm, gathered_hbm,
    out_ref, over_ref, q_ref, kv, far, mine, acc, lengths_ref,
    q_sem, own_sem, lengths_sem, recv_sem, sib_recv, send_sem, sib_send, keep_sem, out_sem,
):
    seq, head = lax.axis_index("seq"), lax.axis_index("head")
    core = seq % 2
    chip = seq // 2
    z = chip % 8
    high = chip // 8
    own = 2 * chip + core

    def device(flip, move, core):
        side = high + flip - 2 * high * flip
        return (side * 16 + ((z + move + 8) % 8) * 2 + core, head)

    sibling = device(0, 0, 1 - core)
    barrier = pltpu.get_barrier_semaphore()
    partners = sorted({(m, f) for m, f in EDGES} | {(-m, f) for m, f in EDGES})
    for move, flip in partners:
        pl.semaphore_signal(barrier, inc=1, device_id=device(flip, move, core), device_id_type=MESH)
    pl.semaphore_signal(barrier, inc=1, device_id=sibling, device_id_type=MESH)

    load_lengths = pltpu.make_async_copy(lengths_hbm, lengths_ref, lengths_sem)
    load_lengths.start()
    for half in range(2):
        part = pl.ds(half * HALF, HALF)
        pltpu.make_async_copy(keys_hbm.at[part], kv.at[own, half, 0], own_sem).start()
        pltpu.make_async_copy(values_hbm.at[part], kv.at[own, half, 1], own_sem).start()
    load_q = pltpu.make_async_copy(queries_hbm, q_ref, q_sem)
    load_q.start()

    ins = [pick(row, chip, 0) for row in IN_WORDS]
    outs = [pick(row, chip, 0) for row in OUT_WORDS]
    works = [pick(row, chip, 0) for row in WORK_WORDS]

    load_lengths.wait()
    lane = lax.broadcasted_iota(jnp.int32, (1, DH), 1)
    first = jnp.zeros((1, DH), jnp.int32)
    last = jnp.zeros((1, DH), jnp.int32)
    begin = jnp.int32(0)
    for number in range(NDOC):
        end = begin + lengths_ref[number]
        first = jnp.where(lane == number, begin, first)
        last = jnp.where(lane == number, end, last)
        begin = end
    row_pos = own * ROWS + lax.broadcasted_iota(jnp.int32, (ROWS, DH), 0)
    mark = ((row_pos >= first) & (row_pos < last)).astype(jnp.float32)
    mine[0] = mark.astype(jnp.bfloat16)
    low = jnp.where(lane < NDOC, first, 0)
    top_pos = jnp.where(lane < NDOC, last, 2 * ROWS * CHIPS)

    @pl.loop(jnp.maximum(chip - REACH, 0), chip + 1)
    def _(block):
        for side in range(2):
            for half in range(2):
                at = block * 2 * ROWS + side * ROWS + half * HALF
                pos = at + lax.broadcasted_iota(jnp.int32, (HALF, DH), 0)
                inside = (pos >= low) & (pos < top_pos)
                away = jnp.where(inside, (lane == NDOC).astype(jnp.float32), FAR)
                far[block, half, side] = away.astype(jnp.bfloat16)

    pltpu.make_async_copy(kv.at[own], kv.at[own], own_sem).wait()
    pl.semaphore_wait(barrier, len(partners) + 1)

    def sib_copy(item, side, sem):
        part = kv.at[2 * (item // 2) + side, item % 2]
        return pltpu.make_async_remote_copy(
            src_ref=part, dst_ref=part, send_sem=sem, recv_sem=sib_recv.at[item],
            device_id=sibling, device_id_type=MESH,
        )

    def edge_copy(item, target, sem):
        part = kv.at[2 * (item // 2) + core, item % 2]
        return pltpu.make_async_remote_copy(
            src_ref=part, dst_ref=part, send_sem=sem, recv_sem=recv_sem.at[item],
            device_id=target, device_id_type=MESH,
        )

    def receive(step, word):
        arrive, needed = (word // 2**15) % 4, word // 2**17
        for place in range(3):
            item = (word // 32**place) % 32

            @pl.when(place < arrive)
            def _():
                edge_copy(item, sibling, send_sem.at[0, 0]).wait_recv()

            @pl.when(place < needed)
            def _():
                sib_copy(item, core, sib_send.at[item]).start()

    def forward(step, word):
        for place in range(3):
            entry = (word // 512**place) % 512
            edge = entry // 32

            @pl.when(place < word // 512**3)
            def _():
                target = device(edge // 5, edge % 5 - 2, core)
                edge_copy(entry % 32, target, send_sem.at[step, place]).start()

    def keep(item, sem):
        at = (pl.ds(2 * (item // 2), 2), item % 2)
        return pltpu.make_async_copy(kv.at[at], gathered_hbm.at[at], sem)

    def settle(step, word):
        for place in range(3):
            @pl.when(place < word // 512**3)
            def _():
                edge_copy(own, sibling, send_sem.at[step, place]).wait_send()

    for step in range(FIRST):
        forward(step, outs[step])
    for half in range(2):
        sib_copy(2 * chip + half, core, sib_send.at[2 * chip + half]).start()

    def load_keys(item):
        both = kv[pl.ds(2 * (item // 2), 2), item % 2, 0].reshape(ROWS, DH)
        away = far[item // 2, item % 2].reshape(ROWS, DH)
        return jnp.concatenate([both, away], axis=1)

    def load_values(item):
        both = kv[pl.ds(2 * (item // 2), 2), item % 2, 1].reshape(ROWS, DH)
        return jnp.concatenate([both, jnp.ones_like(both)], axis=1)

    def load_queries(h, which):
        return jnp.concatenate([q_ref[:, h * DH:(h + 1) * DH], mine[which]], axis=1)

    def product(h, which, keys):
        return lax.dot_general(load_queries(h, which), keys, NT, preferred_element_type=jnp.float32)

    def absorb(items):
        keys = jnp.concatenate([load_keys(item) for item in items], axis=0)
        values = jnp.concatenate([load_values(item) for item in items], axis=0)
        weights = None
        for h in range(HQ + 1):
            ready = weights
            if h < HQ:
                weights = jnp.exp2(product(h, h + 1, keys) * SCALE).astype(jnp.bfloat16)
            if h >= 1:
                acc[h - 1] += jnp.dot(ready, values, preferred_element_type=jnp.float32)

    load_q.wait()
    for half in range(2):
        sib_copy(2 * chip + half, 1 - core, sib_send.at[0]).wait_recv()
    shape = (ROWS, 2 * ROWS)
    column = lax.broadcasted_iota(jnp.int32, shape, 1)
    column = (column // ROWS) * HALF + ((column // HALF) % 2) * ROWS + column % HALF
    causal = column <= core * ROWS + lax.broadcasted_iota(jnp.int32, shape, 0)
    items = [2 * chip, 2 * chip + 1]
    for half in range(2):
        keep(items[half], keep_sem.at[items[half]]).start()
    keys = jnp.concatenate([load_keys(item) for item in items], axis=0)
    values = jnp.concatenate([load_values(item) for item in items], axis=0)
    for h in range(HQ):
        scores = jnp.where(causal, product(h, 0, keys), -1e30)
        shift = jnp.max(scores, axis=1, keepdims=True).astype(jnp.bfloat16).astype(jnp.float32)
        mine[h + 1] = jnp.where(lane == NDOC, -shift, mark).astype(jnp.bfloat16)
        weights = jnp.exp2((scores - shift) * SCALE).astype(jnp.bfloat16)
        acc[h] = jnp.dot(weights, values, preferred_element_type=jnp.float32)

    @pl.loop(FIRST, FIRST + 1 + len(WORK_WORDS))
    def _(step):
        arrived = pick(ins, step - FIRST, 0)
        receive(step, arrived)
        forward(step, pick(outs, step, 0))

        word = pick(works, step - 1 - FIRST, 0)
        needed = word // 2**15
        items = [(word // 32**place) % 32 for place in range(3)]
        for place in range(3):
            @pl.when(place < needed)
            def _():
                sib_copy(items[place], 1 - core, sib_send.at[0]).wait_recv()
                keep(items[place], keep_sem.at[items[place]]).start()

        for count in range(1, 4):
            @pl.when(needed == count)
            def _():
                absorb(items[:count])

    def store(h):
        at = (slice(None), pl.ds(h * DH, DH))
        return pltpu.make_async_copy(out_ref.at[at], out_hbm.at[at], out_sem.at[h])

    over = jnp.zeros((ROWS, DH), jnp.float32)
    for h in range(HQ):
        total = acc[h, :, DH:]
        over = jnp.where(total < LIMIT, over, 1.0)
        out_ref[:, h * DH:(h + 1) * DH] = (acc[h, :, :DH] / total).astype(jnp.bfloat16)
        store(h).start()
    over_ref[...] = jnp.max(over.reshape(ROWS // 8, 8, DH), axis=0)
    store_over = pltpu.make_async_copy(over_ref, over_hbm, out_sem.at[HQ])
    store_over.start()

    @pl.loop(2 * jnp.maximum(chip - REACH, 0), 2 * chip + 2)
    def _(item):
        sib_copy(own, core, sib_send.at[item]).wait_send()
        keep(own, keep_sem.at[item]).wait()

    @pl.loop(0, len(OUT_WORDS))
    def _(step):
        settle(step, pick(outs, step, 0))

    for h in range(HQ):
        store(h).wait()
    store_over.wait()


def repair(
    attended_hbm, over_hbm, gathered_hbm, queries_hbm, lengths_hbm, out_hbm,
    over_ref, kv, q_ref, o_ref, top, acc, lengths_ref, sem, over_sem, in_sem, out_sem,
):
    load = pltpu.make_async_copy(over_hbm, over_ref, over_sem)
    load.start()
    def fetch(piece):
        at = pl.ds(piece * PIECE, PIECE)
        return pltpu.make_async_copy(attended_hbm.at[at], o_ref.at[at], in_sem.at[piece])

    def store(piece):
        at = pl.ds(piece * PIECE, PIECE)
        return pltpu.make_async_copy(o_ref.at[at], out_hbm.at[at], out_sem.at[piece])

    for piece in range(ROWS // PIECE):
        fetch(piece).start()
    for piece in range(ROWS // PIECE):
        fetch(piece).wait()
        store(piece).start()
    load.wait()
    over = jnp.max(over_ref[...])
    for piece in range(ROWS // PIECE):
        store(piece).wait()

    @pl.when(over > 0.0)
    def _():
        seq = lax.axis_index("seq")
        chip = seq // 2
        load = pltpu.make_async_copy(gathered_hbm, kv, sem)
        load.start()
        load.wait()
        load = pltpu.make_async_copy(queries_hbm, q_ref, sem)
        load.start()
        load.wait()
        load = pltpu.make_async_copy(lengths_hbm, lengths_ref, sem)
        load.start()
        load.wait()
        shape = (ROWS, ROWS)
        row = seq * ROWS + lax.broadcasted_iota(jnp.int32, shape, 0)
        low = jnp.zeros(shape, jnp.int32)
        begin = jnp.int32(0)
        for number in range(NDOC):
            low = jnp.where(row >= begin, begin, low)
            begin = begin + lengths_ref[number]
        top[...] = jnp.full_like(top, -1e30)
        acc[...] = jnp.zeros_like(acc)

        @pl.loop(2 * jnp.maximum(chip - REACH, 0), seq + 1)
        def _(block):
            key = block * ROWS + lax.broadcasted_iota(jnp.int32, shape, 1)
            allowed = (key >= low) & (key <= row)
            keys = kv[block, :, 0].reshape(ROWS, DH)
            values = kv[block, :, 1].reshape(ROWS, DH)
            values = jnp.concatenate([values, jnp.ones_like(values)], axis=1)
            for h in range(HQ):
                queries = q_ref[:, h * DH:(h + 1) * DH]
                scores = lax.dot_general(queries, keys, NT, preferred_element_type=jnp.float32)
                old = top[h]
                peak = jnp.max(jnp.where(allowed, scores, -1e30), axis=1, keepdims=True)
                new = jnp.maximum(old, peak)
                top[h] = new
                fade = jnp.exp2((old - new) * SCALE)
                both = jnp.concatenate([new, new], axis=1)
                weights = jnp.where(allowed, jnp.exp2((scores - both) * SCALE), 0.0)
                acc[h] = acc[h] * jnp.concatenate([fade, fade], axis=1) + jnp.dot(
                    weights.astype(jnp.bfloat16), values, preferred_element_type=jnp.float32
                )

        for h in range(HQ):
            o_ref[:, h * DH:(h + 1) * DH] = (acc[h, :, :DH] / acc[h, :, DH:]).astype(jnp.bfloat16)
        again = pltpu.make_async_copy(o_ref, out_hbm, sem)
        again.start()
        again.wait()


def local(queries, keys, values, lengths):
    far_away = pl.BlockSpec(memory_space=pltpu.HBM)
    attended, over, gathered = pl.pallas_call(
        kernel,
        out_shape=(
            jax.ShapeDtypeStruct(queries.shape, jnp.bfloat16),
            jax.ShapeDtypeStruct((8, DH), jnp.float32),
            jax.ShapeDtypeStruct((2 * CHIPS, 2, 2, HALF, DH), jnp.bfloat16),
        ),
        in_specs=[far_away] * 4,
        out_specs=(far_away,) * 3,
        scratch_shapes=[
            pltpu.VMEM((ROWS, HQ * DH), jnp.bfloat16),
            pltpu.VMEM((8, DH), jnp.float32),
            pltpu.VMEM((ROWS, HQ * DH), jnp.bfloat16),
            pltpu.VMEM((2 * CHIPS, 2, 2, HALF, DH), jnp.bfloat16),
            pltpu.VMEM((CHIPS, 2, 2, HALF, DH), jnp.bfloat16),
            pltpu.VMEM((HQ + 1, ROWS, DH), jnp.bfloat16),
            pltpu.VMEM((HQ, ROWS, 2 * DH), jnp.float32),
            pltpu.SMEM((NDOC,), jnp.int32),
            pltpu.SemaphoreType.DMA,
            pltpu.SemaphoreType.DMA,
            pltpu.SemaphoreType.DMA,
            pltpu.SemaphoreType.DMA((2 * CHIPS,)),
            pltpu.SemaphoreType.DMA((2 * CHIPS,)),
            pltpu.SemaphoreType.DMA((len(OUT_WORDS), 3)),
            pltpu.SemaphoreType.DMA((2 * CHIPS,)),
            pltpu.SemaphoreType.DMA((2 * CHIPS,)),
            pltpu.SemaphoreType.DMA((HQ + 1,)),
        ],
        compiler_params=pltpu.CompilerParams(
            collective_id=0, has_side_effects=True, vmem_limit_bytes=60 * 2**20
        ),
    )(queries, keys, values, lengths)
    return pl.pallas_call(
        repair,
        out_shape=jax.ShapeDtypeStruct(queries.shape, jnp.bfloat16),
        in_specs=[far_away] * 5,
        out_specs=far_away,
        scratch_shapes=[
            pltpu.VMEM((8, DH), jnp.float32),
            pltpu.VMEM((2 * CHIPS, 2, 2, HALF, DH), jnp.bfloat16),
            pltpu.VMEM((ROWS, HQ * DH), jnp.bfloat16),
            pltpu.VMEM((ROWS, HQ * DH), jnp.bfloat16),
            pltpu.VMEM((HQ, ROWS, DH), jnp.float32),
            pltpu.VMEM((HQ, ROWS, 2 * DH), jnp.float32),
            pltpu.SMEM((NDOC,), jnp.int32),
            pltpu.SemaphoreType.DMA,
            pltpu.SemaphoreType.DMA,
            pltpu.SemaphoreType.DMA((ROWS // PIECE,)),
            pltpu.SemaphoreType.DMA((ROWS // PIECE,)),
        ],
        compiler_params=pltpu.CompilerParams(vmem_limit_bytes=60 * 2**20),
    )(attended, over, gathered, queries, lengths)


def solution(mesh):
    placed = (P("seq", "head"), P("seq", "head"), P("seq", "head"), P())
    return jax.shard_map(
        local, mesh=mesh, in_specs=placed, out_specs=P("seq", "head"), check_vma=False
    )
```

time: 362 us -> 32.9 us (0.09); the launches traced: 357 us -> 32.8 us
  waiting for transfers between devices: 161 us -> 0 us
  matrix products: 95.4 us -> 0 us
  other arithmetic: 58.8 us -> 0 us
  Pallas kernels: 0 us -> 32.8 us
  local copies, waits for them, and re-layouts: 16.5 us -> 0 us
  between operations: 13.5 us -> 0.01 us
  loops' own time: 12.1 us -> 0 us
    all_gather x2 -> x0, waiting for transfers between devices: 160 us -> none  [the longest x1 80.2 us: local(): key_piece = lax.all_gather(keys, 'seq', axis=0, tiled=True)]
    dot_general x32 -> x0, matrix products: 95.4 us -> none  [the longest x16 57.7 us: absorb(): jnp.einsum('thd,kd->thk', query_heads, key_block, preferred_element_type=...]
    reduce_sum x33 -> x0, other arithmetic: 52.7 us -> none  [the longest x16 51.2 us: absorb(): total_new = total_old * fade + jnp.sum(weights, axis=2)]
    pallas_call x0 -> x2, Pallas kernels: none -> 32.8 us  [the longest x1 30.9 us: local(): pl.pallas_call(kernel, out_shape=(jax.ShapeDtypeStruct(queries.shape, jnp...]
    another operation x1 -> x0, loops' own time: 12.1 us -> none  [local(): lax.scan(step_block, init, (numbers, key_blocks, value_blocks))]
    dynamic_slice x16 -> x0, local copies, waits for them, and re-layouts: 10.7 us -> none  [local(): lax.scan(step_block, init, (numbers, key_blocks, value_blocks))]
    and x16 -> x0, other arithmetic: 4.33 us -> none  [absorb(): (key_pos[None, :] <= query_pos[:, None]) & (key_doc[None, :] == query_doc...]
  transfers between devices with their start and end apart: 2 -> 0, of which waited for: 2 -> 0; matrix products, arithmetic and copies ran while one was open for 1% -> 0% of each run, Pallas kernels for 0% -> 0%
where the time goes in v2:
time: 32.9 us; the launch traced here: 32.8 us
  Pallas kernels  32.8 us (100%)
    pallas_call x1, Pallas kernels, local(): pl.pallas_call(kernel, out_shape=(jax.ShapeDtypeStruct(queries.shape, jnp...  30.9 us
    pallas_call x1, Pallas kernels, local(): pl.pallas_call(repair, out_shape=jax.ShapeDtypeStruct(queries.shape, jnp....  1.84 us

profile of v2, /device:TPU:23, one launch (start us, length us, event | category | flops | bytes accessed | tf_op | source)
XLA Modules:
  0.0 32.8 jit_solution(257068140874937596)
XLA Ops:
  0.0 30.9 %shard_map.46 = (bf16[256,1024]{1,0:T(8,128)(2,1)}, f32[8,128]{1,0:T(8,128)}, bf16[32,2,2,128,128]{4,3,2,1,0:T(8,128)(2,1)}) custom-call(bf16[256,1024]{1,0:T(8,128)(2,1)} %queries_hbm.3, bf16[256,128]{1,0:T(8,128)(2,1)} %keys_hbm.1, bf16[256,128]{1,0:T(8,128)(2,1)} %values_hbm.1, s32[16]{0:T(128)} %lengths_hbm.3), custom_call_target="tpu_custom_call" | custom-call | tf_op jit(solution)/shard_map/pallas_call | solution.py:358
  30.9 1.8 %shard_map.47 = bf16[256,1024]{1,0:T(8,128)(2,1)} custom-call(bf16[256,1024]{1,0:T(8,128)(2,1)} %get-tuple-element.8.attended_hbm, f32[8,128]{1,0:T(8,128)} %get-tuple-element.9.over_hbm, bf16[32,2,2,128,128]{4,3,2,1,0:T(8,128)(2,1)} %get-tuple-element.10.gathered_hbm, bf16[256,1024]{1,0:T(8,128)(2,1)} %queries_hbm.3, s32[16]{0:T(128)} %lengths_hbm.3), custom_call_target="tpu_custom_call" | custom-call | tf_op jit(solution)/shard_map/pallas_call | solution.py:390

commit v3 on v2

--- a/solution.py
+++ b/solution.py
@@ -17,8 +17,8 @@
 FAR = -(2.0**20)
 SCALE = math.log2(math.e) / math.sqrt(DH)
 REACH = 9
+BEHIND = 4
 LIMIT = 2.0**100
-PIECE = 64
 
 FIRST = 3
 WORK_WORDS = (
@@ -69,9 +69,9 @@
 
 
 def kernel(
-    queries_hbm, keys_hbm, values_hbm, lengths_hbm, out_hbm, over_hbm, gathered_hbm,
-    out_ref, over_ref, q_ref, kv, far, mine, acc, lengths_ref,
-    q_sem, own_sem, lengths_sem, recv_sem, sib_recv, send_sem, sib_send, keep_sem, out_sem,
+    queries_hbm, keys_hbm, values_hbm, lengths_hbm, out_ref, over_ref, gathered_hbm,
+    q_ref, kv, far, mine, acc, lengths_ref,
+    q_sem, own_sem, lengths_sem, recv_sem, sib_recv, send_sem, sib_send, keep_sem,
 ):
     seq, head = lax.axis_index("seq"), lax.axis_index("head")
     core = seq % 2
@@ -158,7 +158,7 @@
 
             @pl.when(place < needed)
             def _():
-                sib_copy(item, core, sib_send.at[item]).start()
+                sib_copy(item, core, sib_send).start()
 
     def forward(step, word):
         for place in range(3):
@@ -183,7 +183,7 @@
     for step in range(FIRST):
         forward(step, outs[step])
     for half in range(2):
-        sib_copy(2 * chip + half, core, sib_send.at[2 * chip + half]).start()
+        sib_copy(2 * chip + half, core, sib_send).start()
 
     def load_keys(item):
         both = kv[pl.ds(2 * (item // 2), 2), item % 2, 0].reshape(ROWS, DH)
@@ -197,38 +197,39 @@
     def load_queries(h, which):
         return jnp.concatenate([q_ref[:, h * DH:(h + 1) * DH], mine[which]], axis=1)
 
-    def product(h, which, keys):
+    def product(h, which, items):
+        keys = jnp.concatenate([load_keys(item) for item in items], axis=0)
         return lax.dot_general(load_queries(h, which), keys, NT, preferred_element_type=jnp.float32)
 
+    def mix(weights, items):
+        values = jnp.concatenate([load_values(item) for item in items], axis=0)
+        return jnp.dot(weights, values, preferred_element_type=jnp.float32)
+
     def absorb(items):
-        keys = jnp.concatenate([load_keys(item) for item in items], axis=0)
-        values = jnp.concatenate([load_values(item) for item in items], axis=0)
         weights = None
         for h in range(HQ + 1):
             ready = weights
             if h < HQ:
-                weights = jnp.exp2(product(h, h + 1, keys) * SCALE).astype(jnp.bfloat16)
+                weights = jnp.exp2(product(h, h + 1, items) * SCALE).astype(jnp.bfloat16)
             if h >= 1:
-                acc[h - 1] += jnp.dot(ready, values, preferred_element_type=jnp.float32)
+                acc[h - 1] += mix(ready, items)
 
     load_q.wait()
     for half in range(2):
-        sib_copy(2 * chip + half, 1 - core, sib_send.at[0]).wait_recv()
+        sib_copy(2 * chip + half, 1 - core, sib_send).wait_recv()
     shape = (ROWS, 2 * ROWS)
     column = lax.broadcasted_iota(jnp.int32, shape, 1)
     column = (column // ROWS) * HALF + ((column // HALF) % 2) * ROWS + column % HALF
     causal = column <= core * ROWS + lax.broadcasted_iota(jnp.int32, shape, 0)
     items = [2 * chip, 2 * chip + 1]
     for half in range(2):
-        keep(items[half], keep_sem.at[items[half]]).start()
-    keys = jnp.concatenate([load_keys(item) for item in items], axis=0)
-    values = jnp.concatenate([load_values(item) for item in items], axis=0)
+        keep(items[half], keep_sem).start()
     for h in range(HQ):
-        scores = jnp.where(causal, product(h, 0, keys), -1e30)
+        scores = jnp.where(causal, product(h, 0, items), -1e30)
         shift = jnp.max(scores, axis=1, keepdims=True).astype(jnp.bfloat16).astype(jnp.float32)
         mine[h + 1] = jnp.where(lane == NDOC, -shift, mark).astype(jnp.bfloat16)
         weights = jnp.exp2((scores - shift) * SCALE).astype(jnp.bfloat16)
-        acc[h] = jnp.dot(weights, values, preferred_element_type=jnp.float32)
+        acc[h] = mix(weights, items)
 
     @pl.loop(FIRST, FIRST + 1 + len(WORK_WORDS))
     def _(step):
@@ -236,71 +237,52 @@
         receive(step, arrived)
         forward(step, pick(outs, step, 0))
 
+        settle(step - BEHIND, pick(outs, step - BEHIND, 0))
+
         word = pick(works, step - 1 - FIRST, 0)
         needed = word // 2**15
         items = [(word // 32**place) % 32 for place in range(3)]
         for place in range(3):
             @pl.when(place < needed)
             def _():
-                sib_copy(items[place], 1 - core, sib_send.at[0]).wait_recv()
-                keep(items[place], keep_sem.at[items[place]]).start()
+                sib_copy(items[place], 1 - core, sib_send).wait_recv()
+                keep(items[place], keep_sem).start()
 
         for count in range(1, 4):
             @pl.when(needed == count)
             def _():
                 absorb(items[:count])
-
-    def store(h):
-        at = (slice(None), pl.ds(h * DH, DH))
-        return pltpu.make_async_copy(out_ref.at[at], out_hbm.at[at], out_sem.at[h])
 
     over = jnp.zeros((ROWS, DH), jnp.float32)
     for h in range(HQ):
         total = acc[h, :, DH:]
         over = jnp.where(total < LIMIT, over, 1.0)
         out_ref[:, h * DH:(h + 1) * DH] = (acc[h, :, :DH] / total).astype(jnp.bfloat16)
-        store(h).start()
     over_ref[...] = jnp.max(over.reshape(ROWS // 8, 8, DH), axis=0)
-    store_over = pltpu.make_async_copy(over_ref, over_hbm, out_sem.at[HQ])
-    store_over.start()
-
-    @pl.loop(2 * jnp.maximum(chip - REACH, 0), 2 * chip + 2)
-    def _(item):
-        sib_copy(own, core, sib_send.at[item]).wait_send()
-        keep(own, keep_sem.at[item]).wait()
-
-    @pl.loop(0, len(OUT_WORDS))
-    def _(step):
-        settle(step, pick(outs, step, 0))
-
-    for h in range(HQ):
-        store(h).wait()
-    store_over.wait()
+
+    for step in range(FIRST + 1 + len(WORK_WORDS) - BEHIND, len(OUT_WORDS)):
+        settle(step, outs[step])
+
+    for count in range(1, REACH + 2):
+        @pl.when(jnp.minimum(chip, REACH) + 1 == count)
+        def _():
+            blocks = kv.at[pl.ds(0, count)]
+            pltpu.make_async_remote_copy(
+                src_ref=blocks, dst_ref=blocks, send_sem=sib_send, recv_sem=sib_recv.at[0],
+                device_id=sibling, device_id_type=MESH,
+            ).wait_send()
+            kept = pl.ds(0, 2 * count)
+            pltpu.make_async_copy(kv.at[kept], gathered_hbm.at[kept], keep_sem).wait()
 
 
 def repair(
-    attended_hbm, over_hbm, gathered_hbm, queries_hbm, lengths_hbm, out_hbm,
-    over_ref, kv, q_ref, o_ref, top, acc, lengths_ref, sem, over_sem, in_sem, out_sem,
+    attended_ref, over_ref, gathered_hbm, queries_hbm, lengths_hbm, out_hbm,
+    kv, q_ref, o_ref, top, acc, lengths_ref, sem,
 ):
-    load = pltpu.make_async_copy(over_hbm, over_ref, over_sem)
-    load.start()
-    def fetch(piece):
-        at = pl.ds(piece * PIECE, PIECE)
-        return pltpu.make_async_copy(attended_hbm.at[at], o_ref.at[at], in_sem.at[piece])
-
-    def store(piece):
-        at = pl.ds(piece * PIECE, PIECE)
-        return pltpu.make_async_copy(o_ref.at[at], out_hbm.at[at], out_sem.at[piece])
-
-    for piece in range(ROWS // PIECE):
-        fetch(piece).start()
-    for piece in range(ROWS // PIECE):
-        fetch(piece).wait()
-        store(piece).start()
-    load.wait()
+    copy = pltpu.make_async_copy(attended_ref, out_hbm, sem)
+    copy.start()
     over = jnp.max(over_ref[...])
-    for piece in range(ROWS // PIECE):
-        store(piece).wait()
+    copy.wait()
 
     @pl.when(over > 0.0)
     def _():
@@ -355,18 +337,17 @@
 
 def local(queries, keys, values, lengths):
     far_away = pl.BlockSpec(memory_space=pltpu.HBM)
+    near = pl.BlockSpec(memory_space=pltpu.VMEM)
     attended, over, gathered = pl.pallas_call(
         kernel,
         out_shape=(
-            jax.ShapeDtypeStruct(queries.shape, jnp.bfloat16),
-            jax.ShapeDtypeStruct((8, DH), jnp.float32),
+            pltpu.VMEM(queries.shape, jnp.bfloat16),
+            pltpu.VMEM((8, DH), jnp.float32),
             jax.ShapeDtypeStruct((2 * CHIPS, 2, 2, HALF, DH), jnp.bfloat16),
         ),
         in_specs=[far_away] * 4,
-        out_specs=(far_away,) * 3,
+        out_specs=(near, near, far_away),
         scratch_shapes=[
-            pltpu.VMEM((ROWS, HQ * DH), jnp.bfloat16),
-            pltpu.VMEM((8, DH), jnp.float32),
             pltpu.VMEM((ROWS, HQ * DH), jnp.bfloat16),
             pltpu.VMEM((2 * CHIPS, 2, 2, HALF, DH), jnp.bfloat16),
             pltpu.VMEM((CHIPS, 2, 2, HALF, DH), jnp.bfloat16),
@@ -379,21 +360,19 @@
             pltpu.SemaphoreType.DMA((2 * CHIPS,)),
             pltpu.SemaphoreType.DMA((2 * CHIPS,)),
             pltpu.SemaphoreType.DMA((len(OUT_WORDS), 3)),
-            pltpu.SemaphoreType.DMA((2 * CHIPS,)),
-            pltpu.SemaphoreType.DMA((2 * CHIPS,)),
-            pltpu.SemaphoreType.DMA((HQ + 1,)),
+            pltpu.SemaphoreType.DMA,
+            pltpu.SemaphoreType.DMA,
         ],
         compiler_params=pltpu.CompilerParams(
-            collective_id=0, has_side_effects=True, vmem_limit_bytes=60 * 2**20
+            collective_id=0, has_side_effects=True, vmem_limit_bytes=1708 * 2**15
         ),
     )(queries, keys, values, lengths)
     return pl.pallas_call(
         repair,
         out_shape=jax.ShapeDtypeStruct(queries.shape, jnp.bfloat16),
-        in_specs=[far_away] * 5,
+        in_specs=[near] * 2 + [far_away] * 3,
         out_specs=far_away,
         scratch_shapes=[
-            pltpu.VMEM((8, DH), jnp.float32),
             pltpu.VMEM((2 * CHIPS, 2, 2, HALF, DH), jnp.bfloat16),
             pltpu.VMEM((ROWS, HQ * DH), jnp.bfloat16),
             pltpu.VMEM((ROWS, HQ * DH), jnp.bfloat16),
@@ -401,11 +380,8 @@
             pltpu.VMEM((HQ, ROWS, 2 * DH), jnp.float32),
             pltpu.SMEM((NDOC,), jnp.int32),
             pltpu.SemaphoreType.DMA,
-            pltpu.SemaphoreType.DMA,
-            pltpu.SemaphoreType.DMA((ROWS // PIECE,)),
-            pltpu.SemaphoreType.DMA((ROWS // PIECE,)),
         ],
-        compiler_params=pltpu.CompilerParams(vmem_limit_bytes=60 * 2**20),
+        compiler_params=pltpu.CompilerParams(vmem_limit_bytes=1708 * 2**15),
     )(attended, over, gathered, queries, lengths)
 
 

time: 32.9 us -> 31 us (0.942)
  Pallas kernels: 32.8 us -> 30.3 us
  local copies, waits for them, and re-layouts: 0 us -> 0.65 us
    pallas_call x1, Pallas kernels: 30.9 us -> 29.5 us  [local(): pl.pallas_call(kernel, out_shape=(pltpu.VMEM(queries.shape, jnp.bfloat16)...]
    pallas_call x1, Pallas kernels: 1.84 us -> 0.8 us  [local(): pl.pallas_call(repair, out_shape=jax.ShapeDtypeStruct(queries.shape, jnp....]
    unnamed x0 -> x2, local copies, waits for them, and re-layouts: none -> 0.65 us
where the time goes in v3:
time: 31 us; the launch traced here: 30.9 us
  Pallas kernels  30.3 us (98%)
  local copies, waits for them, and re-layouts  0.65 us (2%)
    pallas_call x1, Pallas kernels, local(): pl.pallas_call(kernel, out_shape=(pltpu.VMEM(queries.shape, jnp.bfloat16)...  29.5 us
    pallas_call x1, Pallas kernels, local(): pl.pallas_call(repair, out_shape=jax.ShapeDtypeStruct(queries.shape, jnp....  0.8 us
    unnamed x2, local copies, waits for them, and re-layouts  0.65 us

profile of v3, /device:TPU:23, one launch (start us, length us, event | category | flops | bytes accessed | tf_op | source)
XLA Modules:
  0.0 30.9 jit_solution(13156744815516460224)
XLA Ops:
  0.0 0.0 copy-start
  0.0 0.7 %copy-done = s32[16]{0:T(128)S(1)} copy-done((s32[16]{0:T(128)S(1)}, s32[16]{0:T(128)}, u32[]{:S(2)}) %copy-start) | copy-done | bytes 88
  0.7 29.5 %shard_map.46 = (bf16[256,1024]{1,0:T(8,128)(2,1)S(1)}, f32[8,128]{1,0:T(8,128)S(1)}, bf16[32,2,2,128,128]{4,3,2,1,0:T(8,128)(2,1)}) custom-call(bf16[256,1024]{1,0:T(8,128)(2,1)} %queries_hbm.3, bf16[256,128]{1,0:T(8,128)(2,1)} %keys_hbm.1, bf16[256,128]{1,0:T(8,128)(2,1)} %values_hbm.1, s32[16]{0:T(128)S(1)} %copy-done), custom_call_target="tpu_custom_call" | custom-call | tf_op jit(solution)/shard_map/pallas_call | solution.py:341
  30.1 0.8 %shard_map.47 = bf16[256,1024]{1,0:T(8,128)(2,1)} custom-call(bf16[256,1024]{1,0:T(8,128)(2,1)S(1)} %get-tuple-element.8.attended_ref, f32[8,128]{1,0:T(8,128)S(1)} %get-tuple-element.9.over_ref, bf16[32,2,2,128,128]{4,3,2,1,0:T(8,128)(2,1)} %get-tuple-element.10.gathered_hbm, bf16[256,1024]{1,0:T(8,128)(2,1)} %queries_hbm.3, s32[16]{0:T(128)S(1)} %copy-done), custom_call_target="tpu_custom_call" | custom-call | tf_op jit(solution)/shard_map/pallas_call | solution.py:370
Async XLA Ops:
  0.0 0.7 %copy-start = (s32[16]{0:T(128)S(1)}, s32[16]{0:T(128)}, u32[]{:S(2)}) copy-start(s32[16]{0:T(128)} %lengths_hbm.3) | copy-start | bytes 196

commit v4 on v3

--- a/solution.py
+++ b/solution.py
@@ -120,6 +120,90 @@
     low = jnp.where(lane < NDOC, first, 0)
     top_pos = jnp.where(lane < NDOC, last, 2 * ROWS * CHIPS)
 
+    pltpu.make_async_copy(kv.at[own], kv.at[own], own_sem).wait()
+    pl.semaphore_wait(barrier, len(partners) + 1)
+
+    def sib_copy(item, side, sem):
+        part = kv.at[2 * (item // 2) + side, item % 2]
+        return pltpu.make_async_remote_copy(
+            src_ref=part, dst_ref=part, send_sem=sem, recv_sem=sib_recv.at[item],
+            device_id=sibling, device_id_type=MESH,
+        )
+
+    def edge_copy(item, target, sem):
+        part = kv.at[2 * (item // 2) + core, item % 2]
+        return pltpu.make_async_remote_copy(
+            src_ref=part, dst_ref=part, send_sem=sem, recv_sem=recv_sem.at[item],
+            device_id=target, device_id_type=MESH,
+        )
+
+    def receive(step, word):
+        arrive, needed = (word // 2**15) % 4, word // 2**17
+        for place in range(3):
+            item = (word // 32**place) % 32
+
+            @pl.when(place < arrive)
+            def _():
+                edge_copy(item, sibling, send_sem.at[0, 0]).wait_recv()
+
+            @pl.when(place < needed)
+            def _():
+                sib_copy(item, core, sib_send).start()
+
+    def forward(step, word):
+        for place in range(3):
+            entry = (word // 512**place) % 512
+            edge = entry // 32
+
+            @pl.when(place < word // 512**3)
+            def _():
+                target = device(edge // 5, edge % 5 - 2, core)
+                edge_copy(entry % 32, target, send_sem.at[step, place]).start()
+
+    def keep(item, sem):
+        at = (pl.ds(2 * (item // 2), 2), item % 2)
+        return pltpu.make_async_copy(kv.at[at], gathered_hbm.at[at], sem)
+
+    def settle(step, word):
+        for place in range(3):
+            @pl.when(place < word // 512**3)
+            def _():
+                edge_copy(own, sibling, send_sem.at[step, place]).wait_send()
+
+    for step in range(FIRST):
+        forward(step, outs[step])
+    for half in range(2):
+        sib_copy(2 * chip + half, core, sib_send).start()
+
+    def load_keys(item):
+        both = kv[pl.ds(2 * (item // 2), 2), item % 2, 0].reshape(ROWS, DH)
+        away = far[item // 2, item % 2].reshape(ROWS, DH)
+        return jnp.concatenate([both, away], axis=1)
+
+    def load_values(item):
+        both = kv[pl.ds(2 * (item // 2), 2), item % 2, 1].reshape(ROWS, DH)
+        return jnp.concatenate([both, jnp.ones_like(both)], axis=1)
+
+    def load_queries(h, which):
+        return jnp.concatenate([q_ref[:, h * DH:(h + 1) * DH], mine[which]], axis=1)
+
+    def product(h, which, items):
+        keys = jnp.concatenate([load_keys(item) for item in items], axis=0)
+        return lax.dot_general(load_queries(h, which), keys, NT, preferred_element_type=jnp.float32)
+
+    def mix(weights, items):
+        values = jnp.concatenate([load_values(item) for item in items], axis=0)
+        return jnp.dot(weights, values, preferred_element_type=jnp.float32)
+
+    def absorb(items):
+        weights = None
+        for h in range(HQ + 1):
+            ready = weights
+            if h < HQ:
+                weights = jnp.exp2(product(h, h + 1, items) * SCALE).astype(jnp.bfloat16)
+            if h >= 1:
+                acc[h - 1] += mix(ready, items)
+
     @pl.loop(jnp.maximum(chip - REACH, 0), chip + 1)
     def _(block):
         for side in range(2):
@@ -129,90 +213,6 @@
                 inside = (pos >= low) & (pos < top_pos)
                 away = jnp.where(inside, (lane == NDOC).astype(jnp.float32), FAR)
                 far[block, half, side] = away.astype(jnp.bfloat16)
-
-    pltpu.make_async_copy(kv.at[own], kv.at[own], own_sem).wait()
-    pl.semaphore_wait(barrier, len(partners) + 1)
-
-    def sib_copy(item, side, sem):
-        part = kv.at[2 * (item // 2) + side, item % 2]
-        return pltpu.make_async_remote_copy(
-            src_ref=part, dst_ref=part, send_sem=sem, recv_sem=sib_recv.at[item],
-            device_id=sibling, device_id_type=MESH,
-        )
-
-    def edge_copy(item, target, sem):
-        part = kv.at[2 * (item // 2) + core, item % 2]
-        return pltpu.make_async_remote_copy(
-            src_ref=part, dst_ref=part, send_sem=sem, recv_sem=recv_sem.at[item],
-            device_id=target, device_id_type=MESH,
-        )
-
-    def receive(step, word):
-        arrive, needed = (word // 2**15) % 4, word // 2**17
-        for place in range(3):
-            item = (word // 32**place) % 32
-
-            @pl.when(place < arrive)
-            def _():
-                edge_copy(item, sibling, send_sem.at[0, 0]).wait_recv()
-
-            @pl.when(place < needed)
-            def _():
-                sib_copy(item, core, sib_send).start()
-
-    def forward(step, word):
-        for place in range(3):
-            entry = (word // 512**place) % 512
-            edge = entry // 32
-
-            @pl.when(place < word // 512**3)
-            def _():
-                target = device(edge // 5, edge % 5 - 2, core)
-                edge_copy(entry % 32, target, send_sem.at[step, place]).start()
-
-    def keep(item, sem):
-        at = (pl.ds(2 * (item // 2), 2), item % 2)
-        return pltpu.make_async_copy(kv.at[at], gathered_hbm.at[at], sem)
-
-    def settle(step, word):
-        for place in range(3):
-            @pl.when(place < word // 512**3)
-            def _():
-                edge_copy(own, sibling, send_sem.at[step, place]).wait_send()
-
-    for step in range(FIRST):
-        forward(step, outs[step])
-    for half in range(2):
-        sib_copy(2 * chip + half, core, sib_send).start()
-
-    def load_keys(item):
-        both = kv[pl.ds(2 * (item // 2), 2), item % 2, 0].reshape(ROWS, DH)
-        away = far[item // 2, item % 2].reshape(ROWS, DH)
-        return jnp.concatenate([both, away], axis=1)
-
-    def load_values(item):
-        both = kv[pl.ds(2 * (item // 2), 2), item % 2, 1].reshape(ROWS, DH)
-        return jnp.concatenate([both, jnp.ones_like(both)], axis=1)
-
-    def load_queries(h, which):
-        return jnp.concatenate([q_ref[:, h * DH:(h + 1) * DH], mine[which]], axis=1)
-
-    def product(h, which, items):
-        keys = jnp.concatenate([load_keys(item) for item in items], axis=0)
-        return lax.dot_general(load_queries(h, which), keys, NT, preferred_element_type=jnp.float32)
-
-    def mix(weights, items):
-        values = jnp.concatenate([load_values(item) for item in items], axis=0)
-        return jnp.dot(weights, values, preferred_element_type=jnp.float32)
-
-    def absorb(items):
-        weights = None
-        for h in range(HQ + 1):
-            ready = weights
-            if h < HQ:
-                weights = jnp.exp2(product(h, h + 1, items) * SCALE).astype(jnp.bfloat16)
-            if h >= 1:
-                acc[h - 1] += mix(ready, items)
 
     load_q.wait()
     for half in range(2):

time: 31 us -> 31 us (level)
  no operation moved by 1% of the time
where the time goes in v4:
time: 31 us; the launch traced here: 30.9 us
  Pallas kernels  30.3 us (98%)
  local copies, waits for them, and re-layouts  0.65 us (2%)
    pallas_call x1, Pallas kernels, local(): pl.pallas_call(kernel, out_shape=(pltpu.VMEM(queries.shape, jnp.bfloat16)...  29.5 us
    pallas_call x1, Pallas kernels, local(): pl.pallas_call(repair, out_shape=jax.ShapeDtypeStruct(queries.shape, jnp....  0.8 us
    unnamed x2, local copies, waits for them, and re-layouts  0.65 us

profile of v4, /device:TPU:23, one launch (start us, length us, event | category | flops | bytes accessed | tf_op | source)
XLA Modules:
  0.0 30.9 jit_solution(10073807492656484689)
XLA Ops:
  0.0 0.0 copy-start
  0.0 0.7 %copy-done = s32[16]{0:T(128)S(1)} copy-done((s32[16]{0:T(128)S(1)}, s32[16]{0:T(128)}, u32[]{:S(2)}) %copy-start) | copy-done | bytes 88
  0.7 29.5 %shard_map.46 = (bf16[256,1024]{1,0:T(8,128)(2,1)S(1)}, f32[8,128]{1,0:T(8,128)S(1)}, bf16[32,2,2,128,128]{4,3,2,1,0:T(8,128)(2,1)}) custom-call(bf16[256,1024]{1,0:T(8,128)(2,1)} %queries_hbm.3, bf16[256,128]{1,0:T(8,128)(2,1)} %keys_hbm.1, bf16[256,128]{1,0:T(8,128)(2,1)} %values_hbm.1, s32[16]{0:T(128)S(1)} %copy-done), custom_call_target="tpu_custom_call" | custom-call | tf_op jit(solution)/shard_map/pallas_call | solution.py:341
  30.1 0.8 %shard_map.47 = bf16[256,1024]{1,0:T(8,128)(2,1)} custom-call(bf16[256,1024]{1,0:T(8,128)(2,1)S(1)} %get-tuple-element.8.attended_ref, f32[8,128]{1,0:T(8,128)S(1)} %get-tuple-element.9.over_ref, bf16[32,2,2,128,128]{4,3,2,1,0:T(8,128)(2,1)} %get-tuple-element.10.gathered_hbm, bf16[256,1024]{1,0:T(8,128)(2,1)} %queries_hbm.3, s32[16]{0:T(128)S(1)} %copy-done), custom_call_target="tpu_custom_call" | custom-call | tf_op jit(solution)/shard_map/pallas_call | solution.py:370
Async XLA Ops:
  0.0 0.7 %copy-start = (s32[16]{0:T(128)S(1)}, s32[16]{0:T(128)}, u32[]{:S(2)}) copy-start(s32[16]{0:T(128)} %lengths_hbm.3) | copy-start | bytes 196
